TPU v7x, 256 devices: a whole 4x4x8 slice. The times are simulated.
256 devices in a mesh: node: 32 (over z, y), mp: 8 (over x, core).
Axes of the slice: x: 4, y: 4, z: 8, core: 2. Of those that a mesh axis runs over, the one named last changes fastest.
Arguments:
- queries: bfloat16 [4, 4096, 5120], P(None, 'node', 'mp'), may hold values from -200 to 200
- keys: bfloat16 [4, 4096, 1024], P(None, ('node', 'mp')), may hold values from -8 to 8
- values: bfloat16 [4, 4096, 1024], P(None, ('node', 'mp')), may hold values from -6 to 6
- grad_out: bfloat16 [4, 4096, 5120], P(None, 'node', 'mp'), may hold values from -6 to 6
- lengths: int32 [4, 32], P(None, 'node'), may hold values from 1 to 128, as said below
- parents: int32 [3, 32], P(None, 'node'), may hold values from 0 to 31, as said below
Outputs:
- attended: bfloat16 [4, 4096, 5120], P(None, 'node', 'mp')
- grad_queries: bfloat16 [4, 4096, 5120], P(None, 'node', 'mp')
- grad_keys: bfloat16 [4, 4096, 1024], P(None, ('node', 'mp'))
- grad_values: bfloat16 [4, 4096, 1024], P(None, ('node', 'mp'))
Inputs may be any that keep to these rules, and one draw needn't show every extreme that they name: `lengths`: each node's valid tokens are its leading positions; some node of every level has 128 of them and some node has one. parents[a, j] is the slot at level a of the parent of node j at level a + 1; its remainder on division by 4 - 1 is a.
All inputs are finite; a program needn't handle non-finite values.
Results may differ from a plain program's by a relative error of at most 0.015.
Values may be sent and summed in bfloat16 or wider, within the bound.
A program may use at most 64 MiB of HBM per device.

v0:
```python
import functools
import math

import jax
import jax.numpy as jnp
from jax import lax
from jax.experimental import pallas as pl
from jax.experimental.pallas import tpu as pltpu
from jax.sharding import PartitionSpec as P

HD = 128
SEG = 128
NZ, NY = 8, 4
NODES = NZ * NY
MP = 8
LEVELS = 4
GROUPS = 5
QR = GROUPS * SEG
TOK = SEG // MP
CTX_ROWS = SEG * LEVELS * (LEVELS + 1) // 2
SETS = 24
F32 = jnp.float32
BF16 = jnp.bfloat16
MESH = pl.DeviceIdType.MESH
SCALE = 1.0 / math.sqrt(HD)
EXP2_SCALE = SCALE * math.log2(math.e)
CH = 32
KEY, VALUE = 0, 1
HOP, META, SHARE, GATHER, SCATTER, LAST, BACK = range(7)
REACH = [(4, 3), (3, 4), (4, 3), (3, 4), (4, 3)]
COLS = (2, 1, 3, 0)
STEPS = [(c, i, s) for c in range(5) for i in range(2) for s in range(REACH[c][i])]
AGZ = {(c, i, s + 1): k for k, (c, i, s) in enumerate(x for x in STEPS if x[0] < 4 or x[2])}
RSZ = {x: k for k, x in enumerate(x for x in STEPS if x[0] < 4 or x[2])}
NEAR = [(0, 0), (0, 1), (0, 2), (0, 3), (1, 0), (-1, 0)]
ENDS = [(VALUE, 0), (VALUE, 1), (VALUE, 2), (VALUE, 3), (KEY, 0), (KEY, 4), (KEY, 5)]
HOPS = [(KEY, 0), (VALUE, 0), (VALUE, 4), (VALUE, 5), (KEY, 1), (KEY, 3), (KEY, 2)]


def dot(a, b, ca, cb):
    return lax.dot_general(a, b, (((ca,), (cb,)), ((), ())), preferred_element_type=F32)


def context(level):
    first = SEG * level * (level + 1) // 2
    return first, (level + 1) * SEG


def kernel(q_hbm, k_hbm, v_hbm, do_hbm, len_s, par_s,
           att_hbm, gq_hbm, gk_o, gv_o,
           ksrc, vsrc, qs, dos, kvl, kg, vg, meta, meta_s, set_s,
           kc, vc, st, dp, plow, dsl, att_v, gq_v, term, cbuf, gfin,
           rz, rz0, ry, sy, last, got, rows_out,
           sent, loc_sem, send_sem, meta_rs, a2a_rs, hop_rs, agz_rs, agy_rs, rsz_rs, rsy_rs, end_rs, back_rs):
    n = lax.axis_index("node")
    m = lax.axis_index("mp")
    z = n >> 2
    y = n & (NY - 1)
    own_class = lax.rem(n, LEVELS - 1)
    sources = (ksrc, vsrc)
    results = (gk_o, gv_o)
    gathered = (kg, vg)

    def node(dz, dy):
        up = ((z + dz) & (NZ - 1)) << 2 if dz % NZ else z << 2
        return up | ((y + dy) & (NY - 1) if dy % NY else y)

    def peer(d):
        return (m + d) & (MP - 1)

    def remote(src, dst, ss, rs, to):
        pltpu.make_async_remote_copy(src_ref=src, dst_ref=dst, send_sem=send_sem.at[ss], recv_sem=rs,
                                     device_id=to, device_id_type=MESH).start()

    def to_node(src, dst, ss, rs, target):
        remote(src, dst, ss, rs, {"node": target})

    def to_mp(src, dst, ss, rs, target):
        remote(src, dst, ss, rs, {"mp": target})

    def to_any(src, dst, ss, rs, target, p):
        remote(src, dst, ss, rs, {"node": target, "mp": p})

    def arrived(ref, sem):
        pltpu.make_async_copy(ref, ref, sem).wait()

    def local(src, dst, sem):
        pltpu.make_async_copy(src, dst, sem).start()

    barrier = pltpu.get_barrier_semaphore()
    for d in (4, 3, 5, 2, 6):
        pl.semaphore_signal(barrier, inc=1, device_id={"node": node(d, 0)}, device_id_type=MESH)
    for near in (2, 1, 3, 4, 5, 0):
        for d in (4, 3, 5, 2, 6, 1, 7, 0):
            if near or d:
                pl.semaphore_signal(barrier, inc=1, device_id={"node": node(*NEAR[near]), "mp": peer(d)}, device_id_type=MESH)

    own_tok = pl.ds(m * TOK, TOK)
    own_lanes = pl.ds(m * HD, HD)
    for kv, src in enumerate((k_hbm, v_hbm)):
        local(src, sources[kv], loc_sem.at[kv])
    for g in range(GROUPS):
        lanes = pl.ds(g * HD, HD)
        for i, (src, dst) in enumerate(((q_hbm, qs), (do_hbm, dos))):
            local(src.at[:, :, lanes], dst.at[:, pl.ds(g * SEG, SEG), :], loc_sem.at[2 + i])

    lane = lax.broadcasted_iota(jnp.int32, (1, 128), 1)
    row = jnp.zeros((1, 128), jnp.int32)
    for level in range(LEVELS):
        row = jnp.where(lane == level, len_s[level], row)
    for level in range(LEVELS - 1):
        row = jnp.where(lane == LEVELS + level, par_s[level], row)
    meta[n] = row
    for kv in range(2):
        arrived(sources[kv], loc_sem.at[kv])
    pl.semaphore_wait(barrier, (MP - 1) + (len(NEAR) - 1) * MP + (NZ - 3))

    for kv, near in HOPS:
        dz, dy = NEAR[near]
        dst = gathered[kv].at[n, own_tok]
        for d in range(1, MP):
            p = peer(d)
            to_any(sources[kv].at[own_class, :, pl.ds(p * HD, HD)], dst, HOP, hop_rs.at[HOPS.index((kv, near))], node(dz, dy), p)
        src = sources[kv].at[own_class, :, own_lanes]
        if near:
            to_node(src, dst, HOP, hop_rs.at[HOPS.index((kv, near))], node(dz, dy))
        else:
            local(src, dst, hop_rs.at[HOPS.index((kv, near))])
    for d in range(1, NY):
        to_node(meta.at[n], meta.at[n], META, meta_rs.at[0], node(0, d))
    for kv in range(2):
        for d in range(1, MP):
            p = peer(d)
            to_mp(sources[kv].at[:, :, pl.ds(p * HD, HD)], kvl.at[kv, :, own_tok], SHARE, a2a_rs.at[kv], p)
        local(sources[kv].at[:, :, own_lanes], kvl.at[kv, :, own_tok], a2a_rs.at[kv])

    def hop_wait(kv, near):
        dz, dy = NEAR[near]
        arrived(gathered[kv].at[node(-dz, -dy)], hop_rs.at[HOPS.index((kv, near))])

    def piece(slot, col):
        return gathered[VALUE if col == 4 else KEY].at[slot]

    def ag_z(col, direction, s):
        sign = 1 if direction == 0 else -1
        src = piece(node(-sign * (s - 1), 0 if col == 4 else col), col)
        to_node(src, src, GATHER, agz_rs.at[AGZ[col, direction, s]], node(sign, 0))

    def ag_z_wait(col, direction, s):
        if col == 4 and s == 1:
            hop_wait(VALUE, 4 + direction)
            return
        sign = 1 if direction == 0 else -1
        dst = piece(node(-sign * s, 0 if col == 4 else col), col)
        arrived(dst, agz_rs.at[AGZ[col, direction, s]])

    def ag_y(t):
        src = piece(node(t, 0), 4)
        for d in (2, 1, 3):
            to_node(src, src, GATHER, agy_rs.at[0], node(0, d))

    def gather_start():
        hop_wait(KEY, 0)
        for direction in range(2):
            ag_z(0, direction, 1)
        hop_wait(VALUE, 0)
        ag_y(0)
        for d in (1, 3, 2):
            hop_wait(KEY, d)
            for direction in range(2):
                ag_z(NY - d, direction, 1)

    def gather_round(s):
        for col in (4, 0, 3, 1, 2):
            for direction in range(2):
                reach = REACH[col][direction]
                if s > reach:
                    continue
                ag_z_wait(col, direction, s)
                if s < reach:
                    ag_z(col, direction, s + 1)
                if col == 4:
                    ag_y((-s if direction == 0 else s) % NZ)

    def gather_end():
        arrived(vg.at[pl.ds(0, (NY - 1) * NZ)], agy_rs.at[0])

    def parent(a, slot):
        return meta_s[slot, 0, LEVELS + a]

    def length(level, slot):
        return meta_s[slot, 0, level]

    def limits(level):
        return [length(a, chains[level][a]) for a in range(level)] + [length(level, n)]

    def fill_context(level, kv, dst):
        first, _ = context(level)
        for a in range(level):
            dst[first + a * SEG:first + (a + 1) * SEG, :] = gathered[kv][chains[level][a]]
        dst[first + level * SEG:first + (level + 1) * SEG, :] = kvl[kv, level]

    def live_rows(level):
        return lax.broadcasted_iota(jnp.int32, (SEG, HD), 0) < length(level, n)

    def probabilities(level):
        first, ctx = context(level)
        fill_context(level, KEY, kc)
        live = live_rows(level)
        for g in range(GROUPS):
            rows = slice(g * SEG, (g + 1) * SEG)
            dos[level, rows, :] = jnp.where(live, dos[level, rows, :], jnp.zeros((), BF16))
        span = slice(first, first + ctx)
        st[span, :] = dot(kc[span, :], qs[level], 1, 1)
        limit = limits(level)
        peak = jnp.full((8, QR), -jnp.inf, F32)
        for r in range(0, ctx, CH):
            b, off = r // SEG, r % SEG
            place = lax.broadcasted_iota(jnp.int32, (CH, QR), 0) + off
            ok = place < limit[b]
            if b == level:
                ok = ok & (place <= (lax.broadcasted_iota(jnp.int32, (CH, QR), 1) & (SEG - 1)))
            s = jnp.where(ok, st[first + r:first + r + CH, :], -jnp.inf)
            st[first + r:first + r + CH, :] = s
            for i in range(0, CH, 8):
                peak = jnp.maximum(peak, s[i:i + 8, :])
        peak = jnp.max(peak, axis=0, keepdims=True)
        total = jnp.zeros((8, QR), F32)
        for r in range(first, first + ctx, CH):
            e = jnp.exp2((st[r:r + CH, :] - peak) * EXP2_SCALE)
            st[r:r + CH, :] = e
            for i in range(0, CH, 8):
                total = total + e[i:i + 8, :]
        inv = 1.0 / jnp.sum(total, axis=0, keepdims=True)
        for r in range(first, first + ctx, CH):
            p = st[r:r + CH, :] * inv
            st[r:r + CH, :] = p
            plow[r:r + CH, :] = p.astype(BF16)
        term[VALUE, span, :] = dot(plow[span, :], dos[level], 1, 0)

    def score_grads(level):
        first, ctx = context(level)
        span = slice(first, first + ctx)
        fill_context(level, VALUE, vc)
        dp[:ctx, :] = dot(vc[span, :], dos[level], 1, 1)
        inner = jnp.zeros((8, QR), F32)
        for r in range(0, ctx, CH):
            prod = st[first + r:first + r + CH, :] * dp[r:r + CH, :]
            for i in range(0, CH, 8):
                inner = inner + prod[i:i + 8, :]
        inner = jnp.sum(inner, axis=0, keepdims=True)
        for r in range(0, ctx, CH):
            g = st[first + r:first + r + CH, :] * (dp[r:r + CH, :] - inner)
            dsl[first + r:first + r + CH, :] = g.astype(BF16)
        term[KEY, span, :] = dot(dsl[span, :], qs[level], 1, 0) * SCALE

    def outputs(level):
        first, ctx = context(level)
        span = slice(first, first + ctx)
        live = live_rows(level)
        out_t = dot(vc[span, :], plow[span, :], 0, 0)
        gq_t = dot(kc[span, :], dsl[span, :], 0, 0) * SCALE
        for g in range(GROUPS):
            cols = slice(g * SEG, (g + 1) * SEG)
            att_v[level, :, cols] = jnp.where(live, jnp.transpose(out_t[:, cols]), 0.0).astype(BF16)
            gq_v[level, :, cols] = jnp.transpose(gq_t[:, cols]).astype(BF16)
        for i, (src, dst) in enumerate(((att_v, att_hbm), (gq_v, gq_hbm))):
            local(src.at[level], dst.at[level], loc_sem.at[4 + i])

    def term_sums(kv):
        for a in range(LEVELS - 1):
            names = list(range(a + 1, LEVELS))
            for bits in range(1 << len(names)):
                slot = kv * SETS + a * 8 + (bits << a)
                for r in range(0, SEG, CH):
                    acc = None
                    for i, level in enumerate(names):
                        if bits >> i & 1:
                            start = context(level)[0] + a * SEG + r
                            x = term[kv, start:start + CH, :]
                            acc = x if acc is None else acc + x
                    if acc is None:
                        acc = jnp.zeros((CH, HD), F32)
                    cbuf[slot, r:r + CH, :] = acc.astype(BF16)

    def own_part(target, col):
        return cbuf[(KEY if col == 4 else VALUE) * SETS + set_s[target]].astype(F32)

    def spread(t):
        for d in (2, 1, 3):
            sy[t, d - 1] = own_part(node(t, d), 4).astype(BF16)
            to_node(sy.at[t, d - 1], ry.at[t, d - 1], SCATTER, rsy_rs.at[t], node(0, d))

    def total_b(t):
        acc = own_part(node(t, 0), 4)
        arrived(ry.at[t], rsy_rs.at[t])
        for d in range(1, NY):
            acc = acc + ry[t, d - 1].astype(F32)
        return acc

    def rs_z(col, direction, t, first):
        src = rz0.at[col, direction] if first else rz.at[col, direction, t]
        to_node(src, rz.at[col, direction, t - 1], SCATTER, rsz_rs.at[RSZ[col, direction, t - 1]],
                node(1 if direction == 0 else -1, 0))

    def rs_z_wait(col, direction, t):
        arrived(rz.at[col, direction, t], rsz_rs.at[RSZ[col, direction, t]])

    def last_hop(kv, near, acc):
        dz, dy = NEAR[near]
        last[kv, near] = acc.astype(BF16)
        dst = got.at[kv, near, m]
        for d in range(1, MP):
            p = peer(d)
            to_any(last.at[kv, near, pl.ds(p * TOK, TOK)], dst, LAST, end_rs.at[ENDS.index((kv, near))], node(dz, dy), p)
        src = last.at[kv, near, own_tok]
        if near:
            to_node(src, dst, LAST, end_rs.at[ENDS.index((kv, near))], node(dz, dy))
        else:
            local(src, dst, end_rs.at[ENDS.index((kv, near))])

    def last_sum(kv):
        nears = [near for k, near in ENDS if k == kv]
        for near in nears:
            arrived(got.at[kv, near], end_rs.at[ENDS.index((kv, near))])
        for head in range(MP):
            acc = sum(got[kv, near, head].astype(F32) for near in nears)
            rows_out[kv, :, head * HD:(head + 1) * HD] = acc.astype(BF16)
        local(rows_out.at[kv], results[kv].at[own_class], loc_sem.at[6])

    def chain(col, step):
        for direction in range(2):
            t = REACH[col][direction] - step
            if t < 0 or (col == 4 and t == 0):
                continue
            if step > 0:
                rs_z_wait(col, direction, t)
            if t == 0:
                continue
            rel = t if direction == 0 else -t
            acc = total_b(rel % NZ) if col == 4 else own_part(node(rel, col), col)
            if step > 0:
                acc = acc + rz[col, direction, t].astype(F32)
            if col == 4 and t == 1:
                last_hop(KEY, 4 + direction, acc)
                continue
            if step == 0:
                rz0[col, direction] = acc.astype(BF16)
            else:
                rz[col, direction, t] = acc.astype(BF16)
            rs_z(col, direction, t, step == 0)

    def ring_step(step):
        for col in COLS:
            chain(col, step)

    def ring_turn():
        for col in COLS:
            chain(col, 4)
            acc = own_part(node(0, col), col) + rz[col, 0, 0].astype(F32) + rz[col, 1, 0].astype(F32)
            if col == 0:
                acc = acc + own_term(VALUE, pl.ds(own_start(own_class), SEG))
            last_hop(VALUE, col, acc)

    def spread_turn():
        last_hop(KEY, 0, total_b(0) + own_term(KEY, pl.ds(own_start(own_class), SEG)))

    def send_back(kv, level):
        dst = results[kv].at[level, :, own_lanes]
        for d in range(1, MP):
            p = peer(d)
            to_mp(gfin.at[kv, level, pl.ds(p * TOK, TOK)], dst, BACK, back_rs.at[kv], p)
        local(gfin.at[kv, level, own_tok], dst, back_rs.at[kv])

    def own_term(kv, level_rows):
        return term[kv, level_rows, :]

    def own_start(level):
        return (level * (level + 3) // 2) * SEG

    def finish_own(kv):
        for i in range(1, LEVELS):
            level = lax.rem(own_class + i, LEVELS)
            gfin[kv, level] = own_term(kv, pl.ds(own_start(level), SEG)).astype(BF16)
            send_back(kv, level)

    gather_start()
    my_row = pl.ds(node(0, 0) - y, NY)
    arrived(meta.at[pl.ds(0, NY - 1)], meta_rs.at[0])
    for d in range(1, NZ):
        to_node(meta.at[my_row], meta.at[my_row], META, meta_rs.at[1], node(d, 0))
    gather_round(1)
    gather_round(2)
    arrived(meta.at[pl.ds(0, NODES - NY)], meta_rs.at[1])
    local(meta, meta_s, loc_sem.at[7])
    pltpu.make_async_copy(meta, meta_s, loc_sem.at[7]).wait()
    chains = []
    for level in range(LEVELS):
        links = [None] * level
        slot = n
        for a in reversed(range(level)):
            slot = parent(a, slot)
            links[a] = slot
        chains.append(links)
    for target in range(NODES):
        a = target % (LEVELS - 1)
        slot = jnp.int32(a * 8)
        for level in range(a + 1, LEVELS):
            slot = slot + (chains[level][a] == target).astype(jnp.int32) * (1 << (level - 1))
        set_s[target] = slot
    gather_round(3)
    arrived(qs, loc_sem.at[2])
    arrived(dos, loc_sem.at[3])
    for kv in range(2):
        arrived(kvl.at[kv], a2a_rs.at[kv])
    gather_round(4)
    probabilities(3)
    probabilities(2)
    probabilities(1)
    term_sums(VALUE)
    ring_step(0)
    gather_end()
    score_grads(3)
    score_grads(2)
    score_grads(1)
    term_sums(KEY)
    spread(4)
    spread(5)
    ring_step(1)
    spread(3)
    spread(6)
    chain(4, 0)
    spread(2)
    spread(7)
    probabilities(0)
    ring_step(2)
    chain(4, 1)
    spread(1)
    spread(0)
    finish_own(VALUE)
    score_grads(0)
    ring_step(3)
    chain(4, 2)
    finish_own(KEY)
    outputs(3)
    ring_turn()
    chain(4, 3)
    spread_turn()
    outputs(2)
    outputs(1)
    outputs(0)
    last_sum(VALUE)
    last_sum(KEY)
    for kv in (VALUE, KEY):
        arrived(results[kv].at[pl.ds(0, LEVELS - 1)], back_rs.at[kv])
    arrived(att_v, loc_sem.at[4])
    arrived(gq_v, loc_sem.at[5])
    arrived(rows_out, loc_sem.at[6])
    units = {HOP: len(HOPS) * MP - 2, SHARE: 2 * (MP - 1) * LEVELS, GATHER: 57 * MP, SCATTER: 57 * MP,
             LAST: len(HOPS) * MP - 2, BACK: 2 * (MP - 1) * (LEVELS - 1)}
    for kind, count in units.items():
        arrived(sent.at[pl.ds(0, count)], send_sem.at[kind])
    arrived(meta.at[pl.ds(0, NODES - 1)], send_sem.at[META])


def store(pieces, *refs):
    src, dst, buf, (load_sem, store_sem) = refs[:4], refs[4:8], refs[8:12], refs[12:]

    def part(arrays, piece):
        i, level = piece
        return arrays[i] if level is None else arrays[i].at[level]

    loads = [pltpu.make_async_copy(part(src, p), part(buf, p), load_sem.at[k]) for k, p in enumerate(pieces)]
    stores = [pltpu.make_async_copy(part(buf, p), part(dst, p), store_sem.at[k]) for k, p in enumerate(pieces)]
    for c in loads:
        c.start()
    for a, b in zip(loads, stores):
        a.wait()
        b.start()
    for c in stores:
        c.wait()


def per_device(queries, keys, values, grad_out, lengths, parents):
    hbm = pl.BlockSpec(memory_space=pltpu.HBM)
    smem = pl.BlockSpec(memory_space=pltpu.SMEM)
    dma = pltpu.SemaphoreType.DMA
    vm = pltpu.VMEM
    ctx = LEVELS * SEG
    block = (SEG, HD)
    results = pl.pallas_call(
        kernel,
        out_shape=tuple(jax.ShapeDtypeStruct(x.shape, BF16) for x in (queries, queries, keys, keys)),
        in_specs=[hbm, hbm, hbm, hbm, smem, smem],
        out_specs=(hbm,) * 4,
        scratch_shapes=[
            vm((LEVELS, TOK, MP * HD), BF16), vm((LEVELS, TOK, MP * HD), BF16),
            vm((LEVELS, QR, HD), BF16), vm((LEVELS, QR, HD), BF16),
            vm((2, LEVELS, SEG, HD), BF16), vm((NODES, SEG, HD), BF16), vm((NODES, SEG, HD), BF16),
            vm((NODES, 1, 128), jnp.int32), pltpu.SMEM((NODES, 1, 128), jnp.int32), pltpu.SMEM((NODES,), jnp.int32),
            vm((CTX_ROWS, HD), BF16), vm((CTX_ROWS, HD), BF16),
            vm((CTX_ROWS, QR), F32), vm((ctx, QR), F32), vm((CTX_ROWS, QR), BF16), vm((CTX_ROWS, QR), BF16),
            vm((LEVELS, SEG, QR), BF16), vm((LEVELS, SEG, QR), BF16),
            vm((2, CTX_ROWS, HD), F32), vm((2 * SETS, SEG, HD), BF16), vm((2, LEVELS, SEG, HD), BF16),
            vm((5, 2, 4) + block, BF16), vm((5, 2) + block, BF16),
            vm((NZ, NY - 1) + block, BF16), vm((NZ, NY - 1) + block, BF16),
            vm((2, len(NEAR)) + block, BF16), vm((2, len(NEAR), MP, TOK, HD), BF16), vm((2, TOK, MP * HD), BF16),
            vm((57 * MP, TOK, HD), BF16),
            dma((8,)), dma((7,)), dma((2,)), dma((2,)), dma((len(HOPS),)), dma((len(AGZ),)), dma((1,)),
            dma((len(RSZ),)), dma((NZ,)), dma((len(HOPS),)), dma((2,)),
        ],
        compiler_params=pltpu.CompilerParams(collective_id=0, has_side_effects=True, vmem_limit_bytes=60 << 20),
        name="tree_attention",
    )(queries, keys, values, grad_out, lengths.reshape(LEVELS), parents.reshape(LEVELS - 1))
    pieces = [(i, level) for i in range(2) for level in range(LEVELS)] + [(2, None), (3, None)]
    return tuple(pl.pallas_call(
        functools.partial(store, pieces),
        out_shape=tuple(jax.ShapeDtypeStruct(x.shape, BF16) for x in results),
        in_specs=[hbm] * 4,
        out_specs=(hbm,) * 4,
        scratch_shapes=[vm(x.shape, BF16) for x in results] + [dma((len(pieces),)), dma((len(pieces),))],
        name="store",
    )(*results))


def solution(mesh):
    placed = (
        P(None, "node", "mp"),
        P(None, ("node", "mp"), None),
        P(None, ("node", "mp"), None),
        P(None, "node", "mp"),
        P(None, "node"),
        P(None, "node"),
    )
    return jax.shard_map(
        per_device,
        mesh=mesh,
        in_specs=placed,
        out_specs=(
            P(None, "node", "mp"),
            P(None, "node", "mp"),
            P(None, ("node", "mp"), None),
            P(None, ("node", "mp"), None),
        ),
        check_vma=False,
    )
```

profile of v0, /device:TPU:1, one launch (start us, length us, event | category | flops | bytes accessed | tf_op | source)
XLA Modules:
  0.0 60.1 jit_solution(12799800469791850685)
XLA Ops:
  0.6 57.2 %tree_attention.1 = (bf16[4,128,640]{2,1,0:T(8,128)(2,1)}, bf16[4,128,640]{2,1,0:T(8,128)(2,1)}, bf16[4,16,1024]{2,1,0:T(8,128)(2,1)}, bf16[4,16,1024]{2,1,0:T(8,128)(2,1)}) custom-call(bf16[4,128,640]{2,1,0:T(8,128)(2,1)} %q_hbm.1, bf16[4,16,1024]{2,1,0:T(8,128)(2,1)} %k_hbm.1, bf16[4,16,1024]{2,1,0:T(8,128)(2,1)} %v_hbm.1, bf16[4,128,640]{2,1,0:T(8,128)(2,1)} %do_hbm.1, ...), custom_call_target="tpu_custom_call" | custom-call | tf_op jit(solution)/shard_map/tree_attention/pallas_call | solution.py:491
  57.8 2.3 %store.1 = (bf16[4,128,640]{2,1,0:T(8,128)(2,1)}, bf16[4,128,640]{2,1,0:T(8,128)(2,1)}, bf16[4,16,1024]{2,1,0:T(8,128)(2,1)}, bf16[4,16,1024]{2,1,0:T(8,128)(2,1)}) custom-call(bf16[4,128,640]{2,1,0:T(8,128)(2,1)} %get-tuple-element.8.refs_0_, bf16[4,128,640]{2,1,0:T(8,128)(2,1)} %get-tuple-element.9.refs_1_, ...), custom_call_target="tpu_custom_call" | custom-call | tf_op jit(solution)/shard_map/store/pallas_call | solution.py:516
where the time goes:
time: 60.3 us; the launch traced here: 60.1 us
  Pallas kernels  59.5 us (99%)
  between operations  0.64 us (1%)
    pallas_call x1, Pallas kernels, per_device(): pl.pallas_call(kernel, out_shape=tuple((jax.ShapeDtypeStruct(x.shape, BF1...  57.2 us
    pallas_call x1, Pallas kernels, per_device(): pl.pallas_call(functools.partial(store, pieces), out_shape=tuple((jax.Sha...  2.33 us

commit v1 on v0

--- a/solution.py
+++ b/solution.py
@@ -128,12 +128,6 @@
             local(src, dst, hop_rs.at[HOPS.index((kv, near))])
     for d in range(1, NY):
         to_node(meta.at[n], meta.at[n], META, meta_rs.at[0], node(0, d))
-    for kv in range(2):
-        for d in range(1, MP):
-            p = peer(d)
-            to_mp(sources[kv].at[:, :, pl.ds(p * HD, HD)], kvl.at[kv, :, own_tok], SHARE, a2a_rs.at[kv], p)
-        local(sources[kv].at[:, :, own_lanes], kvl.at[kv, :, own_tok], a2a_rs.at[kv])
-
     def hop_wait(kv, near):
         dz, dy = NEAR[near]
         arrived(gathered[kv].at[node(-dz, -dy)], hop_rs.at[HOPS.index((kv, near))])
@@ -385,6 +379,11 @@
             send_back(kv, level)
 
     gather_start()
+    for kv in range(2):
+        for d in range(1, MP):
+            p = peer(d)
+            to_mp(sources[kv].at[:, :, pl.ds(p * HD, HD)], kvl.at[kv, :, own_tok], SHARE, a2a_rs.at[kv], p)
+        local(sources[kv].at[:, :, own_lanes], kvl.at[kv, :, own_tok], a2a_rs.at[kv])
     my_row = pl.ds(node(0, 0) - y, NY)
     arrived(meta.at[pl.ds(0, NY - 1)], meta_rs.at[0])
     for d in range(1, NZ):

time: 60.3 us -> 60.1 us (level)
  no operation moved by 1% of the time
where the time goes in v1:
time: 60.1 us; the launch traced here: 60 us
  Pallas kernels  59.3 us (99%)
  between operations  0.64 us (1%)
    pallas_call x1, Pallas kernels, per_device(): pl.pallas_call(kernel, out_shape=tuple((jax.ShapeDtypeStruct(x.shape, BF1...  57 us
    pallas_call x1, Pallas kernels, per_device(): pl.pallas_call(functools.partial(store, pieces), out_shape=tuple((jax.Sha...  2.33 us

profile of v1, /device:TPU:1, one launch (start us, length us, event | category | flops | bytes accessed | tf_op | source)
XLA Modules:
  0.0 60.0 jit_solution(1570140960632724335)
XLA Ops:
  0.6 57.0 %tree_attention.1 = (bf16[4,128,640]{2,1,0:T(8,128)(2,1)}, bf16[4,128,640]{2,1,0:T(8,128)(2,1)}, bf16[4,16,1024]{2,1,0:T(8,128)(2,1)}, bf16[4,16,1024]{2,1,0:T(8,128)(2,1)}) custom-call(bf16[4,128,640]{2,1,0:T(8,128)(2,1)} %q_hbm.1, bf16[4,16,1024]{2,1,0:T(8,128)(2,1)} %k_hbm.1, bf16[4,16,1024]{2,1,0:T(8,128)(2,1)} %v_hbm.1, bf16[4,128,640]{2,1,0:T(8,128)(2,1)} %do_hbm.1, ...), custom_call_target="tpu_custom_call" | custom-call | tf_op jit(solution)/shard_map/tree_attention/pallas_call | solution.py:490
  57.7 2.3 %store.1 = (bf16[4,128,640]{2,1,0:T(8,128)(2,1)}, bf16[4,128,640]{2,1,0:T(8,128)(2,1)}, bf16[4,16,1024]{2,1,0:T(8,128)(2,1)}, bf16[4,16,1024]{2,1,0:T(8,128)(2,1)}) custom-call(bf16[4,128,640]{2,1,0:T(8,128)(2,1)} %get-tuple-element.8.refs_0_, bf16[4,128,640]{2,1,0:T(8,128)(2,1)} %get-tuple-element.9.refs_1_, ...), custom_call_target="tpu_custom_call" | custom-call | tf_op jit(solution)/shard_map/store/pallas_call | solution.py:515
